TPU v7x, 256 devices: a whole 4x4x8 slice. The times are simulated.
256 devices in a mesh: outer: 8 (over x_hi, y), inner: 32 (over x_lo, z, core).
Axes of the slice: x: 4 (x_hi: 2, x_lo: 2; x = x_hi * 2 + x_lo), y: 4, z: 8, core: 2. Of those that a mesh axis runs over, the one named last changes fastest.
Arguments:
- queries: bfloat16 [32768, 512], P(('outer', 'inner')), may hold values from -24 to 24
- keys: bfloat16 [32768, 512], P(('outer', 'inner')), may hold values from -24 to 24
- values: bfloat16 [32768, 512], P(('outer', 'inner')), may hold values from -6 to 6
- block_pos: int32 [256], P(('outer', 'inner')), may hold values from 0 to 255, each once
Outputs:
- attended: bfloat16 [32768, 512], P(('outer', 'inner'))
All inputs are finite; a program needn't handle non-finite values.
Results may differ from a plain program's by a relative error of at most 0.009.
Values may be sent and summed in bfloat16 or wider, within the bound.
A program may use at most 192 MiB of HBM per device.

v0:
```python
import jax
import jax.numpy as jnp
from jax import lax
from jax.sharding import PartitionSpec as P

HEADS = 4


def token_positions(blockpos, tok):
    return (blockpos[:, None] * tok + jnp.arange(tok, dtype=jnp.int32)[None, :]).reshape(-1)


def absorb(carry, queries, qpos, keys_part, vals_part, kpos, heads):
    acc, top, total = carry
    rows = queries.shape[0]
    count = keys_part.shape[0]
    width = queries.shape[1]
    head_size = width // heads
    qh = queries.reshape(rows, heads, head_size)
    kh = keys_part.reshape(count, heads, head_size)
    vh = vals_part.reshape(count, heads, head_size)
    scores = jnp.einsum("qhd,khd->hqk", qh, kh, preferred_element_type=jnp.float32) * head_size ** (
        -0.5
    )
    allowed = kpos[None, :] <= qpos[:, None]
    scores = jnp.where(allowed[None], scores, -1e30)
    newtop = jnp.maximum(top, jnp.max(scores, axis=-1))
    weights = jnp.where(allowed[None], jnp.exp(scores - newtop[..., None]), 0.0).astype(
        jnp.bfloat16
    )
    factor = jnp.exp(top - newtop)
    total = jnp.sum(weights.astype(jnp.float32), axis=-1)
    update = jnp.einsum("hqk,khd->qhd", weights, vh, preferred_element_type=jnp.float32)
    acc = acc.reshape(rows, heads, head_size) * factor.T[:, :, None] + update
    return (acc.reshape(rows, width), newtop, total)


def visit(carry, queries, qpos, keys_part, vals_part, kpos, heads):
    return absorb(carry, queries, qpos, keys_part, vals_part, kpos, heads)


def shards(queries, keys, values, block_pos):
    tok = queries.shape[0]
    width = queries.shape[1]
    heads = HEADS
    head_size = width // heads
    q_group, qblocks = (
        lax.all_gather(queries, "outer", axis=0, tiled=True),
        lax.all_gather(block_pos, "outer", axis=0, tiled=True),
    )
    groups = qblocks.shape[0]
    rows = q_group.shape[0]
    qpos = token_positions(qblocks, tok)
    init = (
        jnp.zeros((rows, width), jnp.float32),
        jnp.full((heads, rows), -1e30, jnp.float32),
        jnp.zeros((heads, rows), jnp.float32),
    )
    keys_part = lax.all_gather(keys, "inner", axis=0, tiled=True)
    vals_part = lax.all_gather(values, "inner", axis=0, tiled=True)
    kblocks = lax.all_gather(block_pos, "inner", axis=0, tiled=True)
    kpos = token_positions(kblocks, tok)
    acc, top, total = visit(init, q_group, qpos, keys_part, vals_part, kpos, heads)
    acc_parts = acc.reshape(groups, tok, width)
    top_parts = top.reshape(heads, groups, tok).transpose(1, 0, 2)
    total_parts = total.reshape(heads, groups, tok).transpose(1, 0, 2)
    acc_parts, top_parts, total_parts = (
        lax.all_to_all(acc_parts, "outer", split_axis=0, concat_axis=0, tiled=True),
        lax.all_to_all(top_parts, "outer", split_axis=0, concat_axis=0, tiled=True),
        lax.all_to_all(total_parts, "outer", split_axis=0, concat_axis=0, tiled=True),
    )
    best = jnp.max(top_parts, axis=0)
    factor = jnp.exp(top_parts - best[None])
    denom = jnp.sum(total_parts * factor, axis=0)
    numer = jnp.sum(
        acc_parts.reshape(groups, tok, heads, head_size) * factor.transpose(0, 2, 1)[..., None],
        axis=0,
    )
    return (numer / denom.T[:, :, None]).reshape(tok, width).astype(jnp.bfloat16)


def solution(mesh):
    return jax.shard_map(
        shards,
        mesh=mesh,
        in_specs=(
            P(("outer", "inner"), None),
            P(("outer", "inner"), None),
            P(("outer", "inner"), None),
            P(("outer", "inner")),
        ),
        out_specs=P(("outer", "inner"), None),
        check_vma=False,
    )
```

profile of v0, /device:TPU:1, one launch (start us, length us, event | category | flops | bytes accessed | tf_op | source)
XLA Modules:
  0.0 283.0 jit_solution(10366601969742707876)
XLA Ops:
  6.5 0.0 all-gather.4.cloned.1.call-start
  6.5 1.6 copy.13
  8.2 0.0 all-gather.4.cloned.1.call-update
  8.2 0.0 all-gather.6.cloned.1.call-start
  8.3 1.7 copy.14
  9.9 0.0 all-gather.6.cloned.1.call-update
  9.9 0.0 all-gather.8.cloned.1.call-start
  10.0 1.7 copy.17
  11.7 0.0 all-gather.8.cloned.1.call-update
  12.3 1.3 dynamic-slice
  13.7 0.7 dynamic-update-slice
  14.4 17.3 %all-reduce = s32[32]{0:T(128)S(1)} all-reduce(s32[32]{0:T(128)S(1)} %dynamic-update-slice), channel_id=1, replica_groups=mesh['outer'=8,'inner'=32] {'inner'}, use_global_device_ids=true, to_apply=%add | all-reduce | flops 32 | bytes 256
  31.7 1.3 dynamic-slice.1
  33.0 0.7 dynamic-update-slice.1
  33.8 0.1 add_bitcast_fusion
  33.8 10.8 %all-reduce.1 = s32[8]{0:T(128)S(1)} all-reduce(s32[8]{0:T(128)S(1)} %dynamic-update-slice.1), channel_id=1, replica_groups=mesh['outer'=8,'inner'=32] {'outer'}, use_global_device_ids=true, to_apply=%add.1 | all-reduce | flops 8 | bytes 64
  44.6 0.1 add_bitcast_fusion.1
  44.7 4.7 %broadcast_compare_fusion = pred[1024,4096]{1,0:T(8,128)(4,1)} fusion(s32[4096]{0:T(1024)S(1)} %add_bitcast_fusion, s32[1024]{0:T(1024)S(1)} %add_bitcast_fusion.1), kind=kLoop, calls=%fused_computation.4 | loop fusion | flops 4194304 | bytes 4214784 | tf_op jit(solution)/shard_map/le | solution.py:25
  49.4 13.8 %all-gather.4.cloned.1.call-done = bf16[1024,512]{0,1:T(8,128)(2,1)} async-done(((bf16[128,512]{0,1:T(8,128)(2,1)}), bf16[1024,512]{0,1:T(8,128)(2,1)}) %all-gather.4.cloned.1.call-update) | async-done | bytes 1048592 | tf_op jit(solution)/shard_map/all_gather | solution.py:48
  63.1 73.6 %all-gather.6.cloned.1.call-done = bf16[4096,512]{0,1:T(8,128)(2,1)} async-done(((bf16[128,512]{0,1:T(8,128)(2,1)}), bf16[4096,512]{0,1:T(8,128)(2,1)}) %all-gather.6.cloned.1.call-update) | async-done | bytes 4194320 | tf_op jit(solution)/shard_map/all_gather | solution.py:59
  136.8 28.0 %fusion = (f32[4,1024]{1,0:T(4,128)S(1)}, f32[4,1024,4096]{2,1,0:T(8,128)}) fusion(pred[1024,4096]{1,0:T(8,128)(4,1)} %broadcast_compare_fusion, bf16[1024,4,128]{0,2,1:T(8,128)(2,1)} %bitcast.45, bf16[4096,4,128]{0,2,1:T(8,128)(2,1)} %bitcast.44), kind=kOutput, calls=%fused_computation.3 | convolution fusion | flops 4345294848 | bytes 76562432 | tf_op jit(solution)/shard_map/qhd,khd->hqk/dot_general | solution.py:22
  164.7 0.6 fusion.4
  165.4 23.4 %convert_reduce_fusion = f32[4,1024]{1,0:T(4,128)S(1)} fusion(f32[4,1024]{1,0:T(4,128)S(1)} %get-tuple-element.9, f32[4,1024,4096]{2,1,0:T(8,128)} %get-tuple-element.11, pred[1024,4096]{1,0:T(8,128)(4,1)} %broadcast_compare_fusion), kind=kLoop, calls=%fused_computation | loop fusion | flops 117436416 | bytes 71335936 | tf_op jit(solution)/shard_map/reduce_sum | solution.py:32
  188.8 12.7 %all_to_all.15 = f32[8,4,128]{2,1,0:T(4,128)S(1)} all-to-all(f32[8,4,128]{2,1,0:T(4,128)S(1)} %bitcast.41), channel_id=1, replica_groups=mesh['outer'=8,'inner'=32] {'outer'}, dimensions={0} | all-to-all | bytes 32768 | tf_op jit(solution)/shard_map/all_to_all | solution.py:70
  201.5 3.5 %all-to-all-start.1 = ((f32[8,4,128]{2,1,0:T(4,128)}), f32[8,4,128]{2,1,0:T(4,128)S(1)}, u32[]{:S(2)}, u32[]{:S(2)}) async-start(f32[8,4,128]{2,1,0:T(4,128)} %get-tuple-element.7), calls=%async_computation.1 | async-start | bytes 32768 | tf_op jit(solution)/shard_map/all_to_all | solution.py:69
  205.0 4.5 %all-gather.8.cloned.1.call-done = bf16[4096,512]{0,1:T(8,128)(2,1)} async-done(((bf16[128,512]{0,1:T(8,128)(2,1)}), bf16[4096,512]{0,1:T(8,128)(2,1)}) %all-gather.8.cloned.1.call-update) | async-done | bytes 4194320 | tf_op jit(solution)/shard_map/all_gather | solution.py:60
  209.5 29.4 %bitcast_add_fusion = f32[1024,4,128]{2,0,1:T(8,128)} fusion(bf16[4096,4,128]{0,2,1:T(8,128)(2,1)} %bitcast.43, f32[1024,4]{0,1:T(4,128)S(1)} %get-tuple-element.8, f32[4,1024,4096]{2,1,0:T(8,128)} %get-tuple-element.11, f32[4,1024]{1,0:T(4,128)S(1)} %get-tuple-element.9, pred[1024,4096]{1,0:T(8,128)(4,1)} %broadcast_compare_fusion), kind=kOutput, calls=%fused_computation.7 | convolution fusion | flops 4379377664 | bytes 77627392 | tf_op jit(solution)/shard_map/hqk,khd->qhd/dot_general | solution.py:33
  238.9 1.9 copy.19
  240.8 0.5 copy.29
  241.3 1.7 copy.20
  243.0 0.0 all-to-all-done.1
  243.0 6.3 %all-to-all-start = ((f32[8,128,512]{1,2,0:T(8,128)}), f32[8,128,512]{1,2,0:T(8,128)S(1)}, u32[]{:S(2)}, u32[]{:S(2)}) async-start(f32[8,128,512]{1,2,0:T(8,128)} %copy.20), calls=%async_computation | async-start | bytes 4194304 | tf_op jit(solution)/shard_map/all_to_all | solution.py:68
  249.4 26.2 %all-to-all-done = f32[8,128,512]{1,2,0:T(8,128)S(1)} async-done(((f32[8,128,512]{1,2,0:T(8,128)}), f32[8,128,512]{1,2,0:T(8,128)S(1)}, u32[]{:S(2)}, u32[]{:S(2)}) %all-to-all-start) | async-done | bytes 2097184 | tf_op jit(solution)/shard_map/all_to_all | solution.py:68
  275.5 0.1 fusion.1
  275.7 0.8 copy.23
  (7 shorter events, 0.1 us)
Async XLA Ops:
  6.5 56.6 %all-gather.4.cloned.1.call-start = ((), (), s32[]{:S(2)}) async-start(), calls=%async_computation.3 | async-start | bytes 1179648 | tf_op jit(solution)/shard_map/all_gather | solution.py:48
  8.2 128.6 %all-gather.6.cloned.1.call-start = ((), (), s32[]{:S(2)}) async-start(), calls=%async_computation.4 | async-start | bytes 4325376 | tf_op jit(solution)/shard_map/all_gather | solution.py:59
  9.9 199.5 %all-gather.8.cloned.1.call-start = ((), (), s32[]{:S(2)}) async-start(), calls=%async_computation.5 | async-start | bytes 4325376 | tf_op jit(solution)/shard_map/all_gather | solution.py:60
  201.5 41.5 %all-to-all-start.1 = ((f32[8,4,128]{2,1,0:T(4,128)}), f32[8,4,128]{2,1,0:T(4,128)S(1)}, u32[]{:S(2)}, u32[]{:S(2)}) async-start(f32[8,4,128]{2,1,0:T(4,128)} %get-tuple-element.7), calls=%async_computation.1 | async-start | bytes 32768 | tf_op jit(solution)/shard_map/all_to_all | solution.py:69
  243.0 32.5 %all-to-all-start = ((f32[8,128,512]{1,2,0:T(8,128)}), f32[8,128,512]{1,2,0:T(8,128)S(1)}, u32[]{:S(2)}, u32[]{:S(2)}) async-start(f32[8,128,512]{1,2,0:T(8,128)} %copy.20), calls=%async_computation | async-start | bytes 4194304 | tf_op jit(solution)/shard_map/all_to_all | solution.py:68
Sparse Core Ops, SparseCore 0:
  9.8 53.2 all-gather.3
  64.9 71.8 all-gather.5
  138.5 70.8 all-gather.7
where the time goes:
time: 283 us
  waiting for transfers between devices  118 us (42%)
  matrix products  57.4 us (20%)
  blocking collectives  40.8 us (14%)
  other arithmetic  29.1 us (10%)
  local copies, waits for them, and re-layouts  14 us (5%)
  between operations  13.8 us (5%)
  starting transfers between devices  9.92 us (4%)
    all_gather x1, waiting for transfers between devices, shards(): keys_part = lax.all_gather(keys, 'inner', axis=0, tiled=True)  73.6 us
    dot_general x1, matrix products, absorb(): jnp.einsum('hqk,khd->qhd', weights, vh, preferred_element_type=jnp.float32)  29.4 us
    unnamed x2, blocking collectives  28.1 us
    dot_general x1, matrix products, absorb(): jnp.einsum('qhd,khd->hqk', qh, kh, preferred_element_type=jnp.float32)  28 us
    all_to_all x1, waiting for transfers between devices, shards(): lax.all_to_all(acc_parts, 'outer', split_axis=0, concat_axis=0, tiled=True)  26.2 us
    reduce_sum x1, other arithmetic, absorb(): total = jnp.sum(weights.astype(jnp.float32), axis=-1)  23.4 us
    all_gather x1, waiting for transfers between devices, shards(): lax.all_gather(queries, 'outer', axis=0, tiled=True)  13.8 us
    all_to_all x1, blocking collectives, shards(): lax.all_to_all(total_parts, 'outer', split_axis=0, concat_axis=0, tiled=T...  12.7 us
  transfers between devices with their start and end apart: 5, of which 4 were waited for; matrix products, arithmetic and copies ran while one was open for 35% of the time, Pallas kernels for 0%

commit v1 on v0

v1 whole, which is shorter than its diff:
```python
import functools

import jax
import jax.numpy as jnp
from jax import lax
from jax.experimental import pallas as pl
from jax.experimental.pallas import tpu as pltpu
from jax.sharding import PartitionSpec as P

TOK = 128
DIM = 128
SUP = 4 * TOK
TQ = 1024
TK = SUP
ROWS = DIM + 16
NQ = 8 * SUP
NK = 8 * SUP
SCALE = DIM**-0.5 * 1.4426950408889634
LOW = -1e30
MESH = pl.DeviceIdType.MESH

OFFSETS = ((0, 0), (0, 1), (0, 3), (0, 2), (1, 0), (1, 1), (1, 3), (1, 2))
BACK = (0, 2, 1, 3, 4, 6, 5, 7)

KEYS_AT = {1: 3, 2: 3, 3: 11, 4: 11, 5: 19, 6: 19, 7: 21}
VALS_AT = {1: 5, 2: 5, 3: 13, 4: 13, 5: 21, 6: 21, 7: 23}
OUTER_SLOTS = 5
TILES = NQ // TQ
LAST_SLOTS = 8 - OUTER_SLOTS
STEPS = 8 * TILES


def kernel(
    q_in, k_in, v_in, p_in, out_ref,
    qall, kall, vall, qpos, kpos, vt, ptile, acc, mx,
    cm_a, cm_b, al_a, al_b, s_a, s_b, p_a, p_b,
    osend, ssend, orecv, srecv, fsend, frecv,
    cell_s, cell_r, ring_s, ring_r, q_s, q_r, o_s, o_r, f_s, f_r,
):
    o, i = lax.axis_index("outer"), lax.axis_index("inner")
    xh, y = o // 4, lax.rem(o, 4)
    xl, z, core = i // 16, lax.rem(i // 2, 8), lax.rem(i, 2)
    me = xl * 2 + core

    def cell(b):
        return (o, (b // 2) * 16 + z * 2 + lax.rem(b, 2))

    def ring(step):
        return (o, xl * 16 + lax.rem(z + step, 8) * 2 + core)

    def group(slot):
        dx, dy = OFFSETS[slot]
        return (lax.rem(xh + dx, 2) * 4 + lax.rem(y + dy, 4), i)

    def lanes(b):
        return pl.ds(pl.multiple_of(b * TOK, TOK), TOK)

    def remote(src, dst, send, recv, device):
        return pltpu.make_async_remote_copy(
            src_ref=src, dst_ref=dst, send_sem=send, recv_sem=recv, device_id=device, device_id_type=MESH
        )

    barrier = pltpu.get_barrier_semaphore()
    partners = [cell(lax.rem(me + j, 4)) for j in (1, 2, 3)] + [ring(1), ring(7)] + [group(s) for s in range(1, 8)]
    for partner in partners:
        pl.semaphore_signal(barrier, inc=1, device_id=partner, device_id_type=MESH)
    ptile[...] = jnp.full(ptile.shape, p_in[0], jnp.int32)
    for h in range(4):
        vt[h * DIM : (h + 1) * DIM, :] = v_in[:, h * DIM : (h + 1) * DIM].T
    pl.semaphore_wait(barrier, len(partners))

    def trade(j, what, block):
        to = lax.rem(me + j, 4)
        src, dst = (
            (k_in.at[:, lanes(to)], kall.at[lanes(block), :]),
            (ptile, kpos.at[:, lanes(block)]),
            (q_in.at[:, lanes(to)], qall.at[lanes(block), :]),
            (vt.at[lanes(to), :], vall.at[pl.ds(0, DIM), lanes(block)]),
        )[what]
        return remote(src, dst, cell_s.at[j - 1, what], cell_r.at[j - 1, what], cell(to))

    for what in range(4):
        for j in (2, 1, 3):
            trade(j, what, me).start()

    own = lanes(me)
    kall[own, :] = k_in[:, own]
    kpos[:, own] = ptile[...]
    qall[own, :] = q_in[:, own]
    vall[0:DIM, own] = vt[own, :]
    vall[DIM:, :] = jnp.ones((ROWS - DIM, NK), jnp.bfloat16)

    def traded(what):
        for j in (1, 2, 3):
            trade(j, what, lax.rem(me + 4 - j, 4)).wait_recv()

    def hop(way, dist, what):
        if way == 0:
            src, dst = (0 if dist == 1 else 2 * dist - 3), 2 * dist - 1
        else:
            src, dst = 2 * (dist - 1), min(2 * dist, 7)
        a, b = slice(src * SUP, (src + 1) * SUP), slice(dst * SUP, (dst + 1) * SUP)
        refs = (
            (kall.at[a, :], kall.at[b, :]),
            (vall.at[0:DIM, a], vall.at[0:DIM, b]),
            (kpos.at[:, a], kpos.at[:, b]),
        )[what]
        return remote(*refs, ring_s.at[way, dist - 1, what], ring_r.at[way, dist - 1, what], ring(1 if way == 0 else 7))

    def arrival(slot):
        if slot == 7:
            return (0, 4), (1, 4)
        way = (slot + 1) % 2
        return ((way, (slot + 1) // 2),) * 2

    def keys_here(slot):
        way, dist = arrival(slot)[0]
        hop(way, dist, 0).wait_recv()
        hop(way, dist, 2).wait_recv()
        if dist < 3 or (dist == 3 and way == 0):
            hop(way, dist + 1, 0).start()
            hop(way, dist + 1, 2).start()

    def vals_here(slot):
        way, dist = arrival(slot)[1]
        hop(way, dist, 1).wait_recv()
        if dist < 3 or (dist == 3 and way == 1):
            hop(way, dist + 1, 1).start()

    def give(slot, at):
        a, b = slice(0, SUP), slice(at * SUP, (at + 1) * SUP)
        device = group(slot)
        return (
            remote(qall.at[a, :], qall.at[b, :], q_s.at[slot, 0], q_r.at[at, 0], device),
            remote(kpos.at[:, a], qpos.at[:, b], q_s.at[slot, 1], q_r.at[at, 1], device),
        )

    traded(0)
    traded(1)
    for way in range(2):
        hop(way, 1, 0).start()
        hop(way, 1, 2).start()
    traded(2)
    for slot in range(1, 8):
        for copy in give(slot, BACK[slot]):
            copy.start()
    traded(3)
    for way in range(2):
        hop(way, 1, 1).start()

    def queries_here(tile):
        for slot in range(tile * 2, tile * 2 + 2):
            if slot > 0:
                for copy in give(slot, slot):
                    copy.wait_recv()

    qpos[:, 0:SUP] = kpos[:, 0:SUP]
    acc[:, SUP:] = jnp.zeros((ROWS, NQ - SUP), jnp.float32)
    mx[:, SUP:] = jnp.full((8, NQ - SUP), LOW, jnp.float32)
    causal = lax.broadcasted_iota(jnp.int32, (TOK, TOK), 0) <= lax.broadcasted_iota(jnp.int32, (TOK, TOK), 1)
    for b in range(4):
        at = slice(b * TOK, (b + 1) * TOK)
        s = lax.dot_general(kall[at, :], qall[at, :], (((1,), (1,)), ((), ())), preferred_element_type=jnp.float32)
        s = jnp.where(causal, s, LOW)
        top = jnp.max(s, axis=0, keepdims=True)
        w = jnp.where(causal, jnp.exp2(s * SCALE - top * SCALE), 0.0).astype(jnp.bfloat16)
        acc[:, at] = jnp.dot(vall[:, at], w, preferred_element_type=jnp.float32)
        mx[:, at] = jnp.broadcast_to(top, (8, TOK))

    S, W, CM, AL = (s_a, s_b), (p_a, p_b), (cm_a, cm_b), (al_a, al_b)
    first = OUTER_SLOTS * TILES

    def place(n):
        m = jnp.maximum(n - first, 0)
        early = n < first
        slot = jnp.where(early, n // TILES, OUTER_SLOTS + lax.rem(m, LAST_SLOTS))
        tile = jnp.where(early, lax.rem(n, TILES), TILES - 1 - m // LAST_SLOTS)
        return pl.multiple_of(slot * TK, TK), pl.multiple_of(tile * TQ, TQ)

    def kept(k0, q0, t, kb):
        kp = kpos[:, pl.ds(k0 + kb * TOK, TOK)]
        return jnp.concatenate([kp] * 4, axis=1) < qpos[:, pl.ds(q0 + t * SUP, SUP)]

    def scores(n, par):
        k0, q0 = place(n)
        for t in range(TQ // SUP):
            s = lax.dot_general(
                kall[pl.ds(k0, TK), :], qall[pl.ds(q0 + t * SUP, SUP), :],
                (((1,), (1,)), ((), ())), preferred_element_type=jnp.float32,
            )
            S[par][:, t * SUP : (t + 1) * SUP] = s
            best = None
            for kb in range(TK // TOK):
                r = jnp.max(s[kb * TOK : (kb + 1) * TOK].reshape(TOK // 8, 8, SUP), axis=0)
                r = jnp.where(kept(k0, q0, t, kb), r, LOW)
                best = r if best is None else jnp.maximum(best, r)
            CM[par][:, t * SUP : (t + 1) * SUP] = best

    def weights(n, par):
        k0, q0 = place(n)
        qs = pl.ds(q0, TQ)
        old = mx[:, qs]
        new = jnp.maximum(old, jnp.max(CM[par][...], axis=0, keepdims=True))
        mx[:, qs] = new
        AL[par][...] = jnp.exp2((old - new) * SCALE)
        top = new * SCALE
        for t in range(TQ // SUP):
            ts = slice(t * SUP, (t + 1) * SUP)
            for kb in range(TK // TOK):
                less = jnp.where(kept(k0, q0, t, kb), top[:, ts], -LOW)
                ks = slice(kb * TOK, (kb + 1) * TOK)
                e = (S[par][ks, ts] * SCALE).reshape(TOK // 8, 8, SUP) - less[None]
                W[par][ks, ts] = jnp.exp2(e).reshape(TOK, SUP).astype(jnp.bfloat16)

    def sums(n, par):
        k0, q0 = place(n)
        for t in range(TQ // SUP):
            ts = slice(t * SUP, (t + 1) * SUP)
            qs = pl.ds(q0 + t * SUP, SUP)
            new = jnp.dot(vall[:, pl.ds(k0, TK)], W[par][:, ts], preferred_element_type=jnp.float32)
            acc[:, qs] = acc[:, qs] * AL[par][:1, ts] + new

    def stats(slot):
        at = slice(slot * SUP, (slot + 1) * SUP)
        m, l = mx[0:1, at], acc[DIM : DIM + 1, at]
        cut = [slice(b * TOK, (b + 1) * TOK) for b in range(4)]
        return jnp.concatenate([m[:, c] for c in cut] + [l[:, c] for c in cut], axis=0)

    def partial(slot, at):
        device = group(slot)
        return (
            remote(osend.at[slot], orecv.at[at], o_s.at[slot, 0], o_r.at[at, 0], device),
            remote(ssend.at[slot], srecv.at[at], o_s.at[slot, 1], o_r.at[at, 1], device),
        )

    def send_partial(tile):
        for slot in (tile * 2 + 1, tile * 2):
            if slot > 0:
                osend[slot] = acc[0:DIM, slot * SUP : (slot + 1) * SUP].astype(jnp.bfloat16)
                ssend[slot] = stats(slot)
                for copy in partial(slot, BACK[slot]):
                    copy.start()

    queries_here(0)
    scores(jnp.int32(0), 0)
    p_b[...] = jnp.zeros_like(p_b)
    al_b[...] = jnp.ones_like(al_b)
    done = {first + (TILES - t) * LAST_SLOTS: t for t in range(1, TILES)}

    def before(n, n_of):
        events = {}
        for slot, at in KEYS_AT.items():
            events.setdefault(at, []).append(functools.partial(keys_here, slot))
        for slot, at in VALS_AT.items():
            events.setdefault(at, []).append(functools.partial(vals_here, slot))
        for tile in range(1, TILES):
            events.setdefault(tile - 1, []).append(functools.partial(queries_here, tile))
        for at, calls in sorted(events.items()):
            if at % 2 == n_of:

                @pl.when(n == at)
                def _(calls=calls):
                    for call in calls:
                        call()

    def after(n, n_of):
        for at, tile in done.items():
            if at % 2 == n_of:

                @pl.when(n == at)
                def _(tile=tile):
                    send_partial(tile)

    def body(pair, carry):
        for par in range(2):
            n = 2 * pair + par
            before(n, par)
            scores(jnp.minimum(n + 1, STEPS - 1), 1 - par)
            weights(n, par)
            sums(jnp.maximum(n - 1, 0), 1 - par)
            after(n, par)
        return carry

    lax.fori_loop(0, STEPS // 2, body, 0)
    sums(jnp.int32(STEPS - 1), 1)
    send_partial(0)

    mine = stats(0)
    for slot in range(1, 8):
        for copy in partial(slot, slot):
            copy.wait_recv()
    all_stats = [mine] + [srecv[slot] for slot in range(1, 8)]
    best = functools.reduce(jnp.maximum, [st[0:4] for st in all_stats])
    factor = [jnp.exp2((st[0:4] - best) * SCALE) for st in all_stats]
    denom = functools.reduce(jnp.add, [st[4:8] * f for st, f in zip(all_stats, factor)])
    factor = [f / denom for f in factor]
    for b in range(4):
        at = slice(b * TOK, (b + 1) * TOK)
        total = acc[0:DIM, at] * factor[0][b : b + 1]
        for slot in range(1, 8):
            total += orecv[slot, :, at].astype(jnp.float32) * factor[slot][b : b + 1]
        fsend[b] = total.T.astype(jnp.bfloat16)

    def home(j, block):
        to = lax.rem(me + j, 4)
        return remote(fsend.at[to], frecv.at[block], f_s.at[j - 1], f_r.at[j - 1], cell(to))

    for j in (2, 1, 3):
        home(j, me).start()
    out_ref[:, own] = fsend[me]
    for j in (1, 2, 3):
        source = lax.rem(me + 4 - j, 4)
        home(j, source).wait_recv()
        out_ref[:, lanes(source)] = frecv[source]

    for j in (1, 2, 3):
        for what in range(4):
            trade(j, what, me).wait_send()
        home(j, me).wait_send()
    for way in range(2):
        for dist in range(1, 5):
            for what in range(3):
                if dist < 4 or (what == 1) == (way == 1):
                    hop(way, dist, what).wait_send()
    for slot in range(1, 8):
        for copy in give(slot, BACK[slot]) + partial(slot, BACK[slot]):
            copy.wait_send()


def shards(queries, keys, values, block_pos):
    bf, f32, i32 = jnp.bfloat16, jnp.float32, jnp.int32
    vmem, dma = pltpu.VMEM, pltpu.SemaphoreType.DMA
    return pl.pallas_call(
        kernel,
        out_shape=jax.ShapeDtypeStruct(queries.shape, bf),
        in_specs=[pl.BlockSpec(memory_space=pltpu.VMEM)] * 3 + [pl.BlockSpec(memory_space=pltpu.SMEM)],
        out_specs=pl.BlockSpec(memory_space=pltpu.VMEM),
        scratch_shapes=[
            vmem((NQ, DIM), bf), vmem((NK, DIM), bf), vmem((ROWS, NK), bf), vmem((8, NQ), i32), vmem((8, NK), i32),
            vmem((4 * DIM, TOK), bf), vmem((8, TOK), i32), vmem((ROWS, NQ), f32), vmem((8, NQ), f32),
            vmem((8, TQ), f32), vmem((8, TQ), f32), vmem((8, TQ), f32), vmem((8, TQ), f32),
            vmem((TK, TQ), f32), vmem((TK, TQ), f32), vmem((TK, TQ), bf), vmem((TK, TQ), bf),
            vmem((8, DIM, SUP), bf), vmem((8, 8, TOK), f32), vmem((8, DIM, SUP), bf), vmem((8, 8, TOK), f32),
            vmem((4, TOK, DIM), bf), vmem((4, TOK, DIM), bf),
            dma((3, 4)), dma((3, 4)), dma((2, 4, 3)), dma((2, 4, 3)), dma((8, 2)), dma((8, 2)), dma((8, 2)), dma((8, 2)),
            dma((3,)), dma((3,)),
        ],
        compiler_params=pltpu.CompilerParams(collective_id=0, has_side_effects=True, vmem_limit_bytes=56 << 20),
        cost_estimate=pl.CostEstimate(flops=NQ * NK * DIM * 4, bytes_accessed=1 << 20, transcendentals=NQ * NK),
        name="attend",
    )(queries, keys, values, block_pos)


def solution(mesh):
    spec = P(("outer", "inner"), None)
    return jax.shard_map(
        shards, mesh=mesh, in_specs=(spec, spec, spec, P(("outer", "inner"))), out_specs=spec, check_vma=False
    )
```

time: 283 us -> 81 us (0.29)
  waiting for transfers between devices: 118 us -> 0 us
  Pallas kernels: 0 us -> 78.6 us
  matrix products: 57.4 us -> 0 us
  blocking collectives: 40.8 us -> 0 us
  other arithmetic: 29.1 us -> 0 us
  between operations: 13.8 us -> 0.66 us
  local copies, waits for them, and re-layouts: 14 us -> 1.57 us
  starting transfers between devices: 9.92 us -> 0 us
    all_gather x3 -> x0, waiting for transfers between devices: 91.8 us -> none  [the longest x1 73.6 us: shards(): keys_part = lax.all_gather(keys, 'inner', axis=0, tiled=True)]
    pallas_call x0 -> x1, Pallas kernels: none -> 78.6 us  [shards(): pl.pallas_call(kernel, out_shape=jax.ShapeDtypeStruct(queries.shape, bf),...]
    dot_general x2 -> x0, matrix products: 57.4 us -> none  [the longest x1 29.4 us: absorb(): jnp.einsum('hqk,khd->qhd', weights, vh, preferred_element_type=jnp.float32)]
    unnamed x2 -> x0, blocking collectives: 28.1 us -> none
    all_to_all x2 -> x0, waiting for transfers between devices: 26.2 us -> none  [the longest x1 26.2 us: shards(): lax.all_to_all(acc_parts, 'outer', split_axis=0, concat_axis=0, tiled=True)]
    reduce_sum x3 -> x0, other arithmetic: 23.6 us -> none  [the longest x1 23.4 us: absorb(): total = jnp.sum(weights.astype(jnp.float32), axis=-1)]
    all_to_all x1 -> x0, blocking collectives: 12.7 us -> none  [shards(): lax.all_to_all(total_parts, 'outer', split_axis=0, concat_axis=0, tiled=T...]
    all_to_all x2 -> x0, starting transfers between devices: 9.83 us -> none  [the longest x1 6.33 us: shards(): lax.all_to_all(acc_parts, 'outer', split_axis=0, concat_axis=0, tiled=True)]
  transfers between devices with their start and end apart: 5 -> 0, of which waited for: 4 -> 0; matrix products, arithmetic and copies ran while one was open for 35% -> 0% of each run, Pallas kernels for 0% -> 0%
where the time goes in v1:
time: 81 us; the launch traced here: 80.8 us
  Pallas kernels  78.6 us (97%)
  local copies, waits for them, and re-layouts  1.57 us (2%)
    pallas_call x1, Pallas kernels, shards(): pl.pallas_call(kernel, out_shape=jax.ShapeDtypeStruct(queries.shape, bf),...  78.6 us

profile of v1, /device:TPU:1, one launch (start us, length us, event | category | flops | bytes accessed | tf_op | source)
XLA Modules:
  0.0 80.8 jit_solution(17201851077739271438)
XLA Ops:
  0.7 78.6 %attend.1 = bf16[128,512]{1,0:T(8,128)(2,1)} custom-call(bf16[128,512]{1,0:T(8,128)(2,1)} %q_in.1, bf16[128,512]{1,0:T(8,128)(2,1)} %k_in.1, bf16[128,512]{1,0:T(8,128)(2,1)} %v_in.1, s32[1]{0:T(128)S(6)} %copy.6.p_in), custom_call_target="tpu_custom_call" | custom-call | flops 8589934592 | bytes 1048576 | tf_op jit(solution)/shard_map/attend/pallas_call | solution.py:333
  79.3 1.6 %copy.7 = bf16[128,512]{1,0:T(8,128)(2,1)} copy(bf16[128,512]{1,0:T(8,128)(2,1)} %attend.1) | data formatting | bytes 262144

commit v2 on v1

v2 whole, which is shorter than its diff:
```python
import functools

import jax
import jax.numpy as jnp
from jax import lax
from jax.experimental import pallas as pl
from jax.experimental.pallas import tpu as pltpu
from jax.sharding import PartitionSpec as P

TOK = 128
DIM = 128
SUP = 4 * TOK
TQ = 1024
TK = 1024
ROWS = DIM + 16
NQ = 8 * SUP
NK = 8 * SUP
SCALE = DIM**-0.5 * 1.4426950408889634
LOW = -1e30
MESH = pl.DeviceIdType.MESH

OFFSETS = ((0, 0), (0, 1), (0, 3), (0, 2), (1, 0), (1, 1), (1, 3), (1, 2))
BACK = (0, 2, 1, 3, 4, 6, 5, 7)

OWN = 7
K_A, V_A, K_B, V_B, POS = range(5)
FRONT = (K_A, V_A, K_B, POS)
RING_AT = {0: ((1, (3,)),), 1: ((2, (0, 1, 2, 4)),), 3: ((2, (3,)),), 5: ((3, (0, 1, 2, 4)),), 6: ((3, (3,)),), 9: ((4, (0, 1, 2, 4)),), 10: ((4, (3,)),)}
QUERY_AT = {0: 1, 3: 2, 5: 3}
DONE_AT = {14: 1, 12: 2, 11: 3}
TILES = NQ // TQ
STEPS = (NK // TK) * TILES


def kernel(
    q_in, k_in, v_in, p_in, out_ref,
    qall, kall, vall, qpos, kpos, vin, vt, ptile, acc, mx,
    cm_a, cm_b, al_a, al_b, s_a, s_b, p_a, p_b,
    osend, ssend, orecv, srecv, fsend, frecv,
    local, cell_s, cell_r, ring_s, ring_r, q_s, q_r, o_s, o_r, f_s, f_r,
):
    o, i = lax.axis_index("outer"), lax.axis_index("inner")
    xh, y = o // 4, lax.rem(o, 4)
    xl, z, core = i // 16, lax.rem(i // 2, 8), lax.rem(i, 2)

    def device(x, c):
        return (o, x * 16 + z * 2 + c)

    mates = {1: (xl, 1 - core), 2: (1 - xl, core), 3: (1 - xl, 1 - core)}
    theirs = {1: 1 - core, 2: 2 + core, 3: 3 - core}
    mine_at = {1: core, 2: 2 + core, 3: 2 + core}

    def ring(step):
        return (o, xl * 16 + lax.rem(z + step, 8) * 2 + core)

    def group(slot):
        dx, dy = OFFSETS[slot]
        return (lax.rem(xh + dx, 2) * 4 + lax.rem(y + dy, 4), i)

    def lanes(b, base=0):
        return pl.ds(pl.multiple_of(base + b * TOK, TOK), TOK)

    def remote(src, dst, send, recv, device):
        return pltpu.make_async_remote_copy(
            src_ref=src, dst_ref=dst, send_sem=send, recv_sem=recv, device_id=device, device_id_type=MESH
        )

    barrier = pltpu.get_barrier_semaphore()
    partners = [device(*mates[j]) for j in (1, 2, 3)] + [ring(1), ring(7)] + [group(s) for s in range(1, 8)]
    for partner in partners:
        pl.semaphore_signal(barrier, inc=1, device_id=partner, device_id_type=MESH)
    head = lanes(xl * 2 + core)
    loads = [
        pltpu.make_async_copy(v_in, vin, local.at[0]),
        pltpu.make_async_copy(k_in.at[:, head], kall.at[lanes(core, OWN * SUP), :], local.at[1]),
        pltpu.make_async_copy(q_in.at[:, head], qall.at[lanes(core), :], local.at[2]),
    ]
    for load in loads:
        load.start()
    ptile[...] = jnp.full(ptile.shape, p_in[0], jnp.int32)
    kpos[:, lanes(core, OWN * SUP)] = ptile[...]
    vall[DIM:, :] = jnp.ones((ROWS - DIM, NK), jnp.bfloat16)
    for load in loads:
        load.wait()
    for h in range(4):
        vt[h * DIM : (h + 1) * DIM, :] = vin[:, h * DIM : (h + 1) * DIM].T
    pl.semaphore_wait(barrier, len(partners))

    def trade(j, what, block):
        x, c = mates[j]
        to = x * 2 + c
        src, dst = (
            (k_in.at[:, lanes(to)], kall.at[lanes(block, OWN * SUP), :]),
            (vt.at[lanes(to), :], vall.at[pl.ds(0, DIM), lanes(block, OWN * SUP)]),
            (q_in.at[:, lanes(to)], qall.at[lanes(block), :]),
            (ptile, kpos.at[:, lanes(block, OWN * SUP)]),
        )[what]
        return remote(src, dst, cell_s.at[j - 1, what], cell_r.at[j - 1, what], device(x, c))

    for what in (0, 1):
        trade(1, what, mine_at[1]).start()
    for what in (3, 0, 2, 1):
        for j in (2, 3):
            trade(j, what, mine_at[j]).start()
        if what > 1:
            trade(1, what, mine_at[1]).start()
    vall[0:DIM, lanes(core, OWN * SUP)] = vt[head, :]

    def hop(way, dist, what):
        src = OWN if dist == 1 else 2 * (dist - 2) + way
        dst = 6 if dist == 4 else 2 * (dist - 1) + way
        lo, hi = ((0, SUP // 2), (0, SUP // 2), (SUP // 2, SUP), (SUP // 2, SUP), (0, SUP))[what]
        a, b = slice(src * SUP + lo, src * SUP + hi), slice(dst * SUP + lo, dst * SUP + hi)
        if what in (K_A, K_B):
            refs = kall.at[a, :], kall.at[b, :]
        elif what in (V_A, V_B):
            refs = vall.at[0:DIM, a], vall.at[0:DIM, b]
        else:
            refs = kpos.at[:, a], kpos.at[:, b]
        return remote(*refs, ring_s.at[way, dist - 1, what], ring_r.at[way, dist - 1, what], ring(1 if way == 0 else 7))

    def goes(way, dist, what):
        return dist < 4 or (dist == 4 and (what in (V_A, V_B)) == (way == 1))

    def arrive(dist, whats):
        for what in whats:
            for way in range(2):
                if goes(way, dist, what):
                    hop(way, dist, what).wait_recv()
                    if goes(way, dist + 1, what):
                        hop(way, dist + 1, what).start()

    def give(slot, at):
        a, b = slice(0, SUP), slice(at * SUP, (at + 1) * SUP)
        ka = slice(OWN * SUP, (OWN + 1) * SUP)
        return (
            remote(qall.at[a, :], qall.at[b, :], q_s.at[slot, 0], q_r.at[at, 0], group(slot)),
            remote(kpos.at[:, ka], qpos.at[:, b], q_s.at[slot, 1], q_r.at[at, 1], group(slot)),
        )

    def give_all(slots):
        for slot in slots:
            for copy in give(slot, BACK[slot]):
                copy.start()

    def traded(what, js):
        for j in js:
            trade(j, what, theirs[j]).wait_recv()

    def send_on(what):
        for way in range(2):
            hop(way, 1, what).start()

    traded(0, (1,))
    send_on(K_A)
    traded(1, (1,))
    send_on(V_A)
    traded(3, (1, 2, 3))
    send_on(POS)
    traded(0, (2, 3))
    send_on(K_B)
    traded(2, (1, 2, 3))
    give_all((2, 1, 3))
    traded(1, (2, 3))
    send_on(V_B)

    def queries_here(tile):
        for slot in range(tile * 2, tile * 2 + 2):
            if slot > 0:
                for copy in give(slot, slot):
                    copy.wait_recv()

    qpos[:, 0:SUP] = kpos[:, OWN * SUP :]
    acc[:, SUP:] = jnp.zeros((ROWS, NQ - SUP), jnp.float32)
    mx[:, SUP:] = jnp.full((8, NQ - SUP), LOW, jnp.float32)
    causal = lax.broadcasted_iota(jnp.int32, (TOK, TOK), 0) <= lax.broadcasted_iota(jnp.int32, (TOK, TOK), 1)
    for b in range(4):
        at = slice(b * TOK, (b + 1) * TOK)
        kat = slice(OWN * SUP + b * TOK, OWN * SUP + (b + 1) * TOK)
        s = lax.dot_general(kall[kat, :], qall[at, :], (((1,), (1,)), ((), ())), preferred_element_type=jnp.float32)
        s = jnp.where(causal, s, LOW)
        top = jnp.max(s, axis=0, keepdims=True)
        w = jnp.where(causal, jnp.exp2(s * SCALE - top * SCALE), 0.0).astype(jnp.bfloat16)
        acc[:, at] = jnp.dot(vall[:, kat], w, preferred_element_type=jnp.float32)
        mx[:, at] = jnp.broadcast_to(top, (8, TOK))

    S, W, CM, AL = (s_a, s_b), (p_a, p_b), (cm_a, cm_b), (al_a, al_b)

    def place(n):
        keys = jnp.where(n < 2, 0, jnp.where(n < 4, 1, jnp.where(n < 5, 0, jnp.where(n < 6, 1, jnp.where(n < 7, 0, jnp.where(n < 8, 1, jnp.where(n < 10, 2, jnp.where(n < 12, 3, jnp.where(n < 13, 2, jnp.where(n < 14, 3, jnp.where(n < 15, 2, 3)))))))))))
        tile = jnp.where(n < 1, 0, jnp.where(n < 2, 1, jnp.where(n < 3, 0, jnp.where(n < 4, 1, jnp.where(n < 6, 2, jnp.where(n < 9, 3, jnp.where(n < 10, 2, jnp.where(n < 11, 3, jnp.where(n < 12, 2, jnp.where(n < 14, 1, 0))))))))))
        return pl.multiple_of(keys * TK, TK), pl.multiple_of(tile * TQ, TQ)

    def kept(k0, q0, t, kb):
        kp = kpos[:, pl.ds(k0 + kb * TOK, TOK)]
        return jnp.concatenate([kp] * 4, axis=1) < qpos[:, pl.ds(q0 + t * SUP, SUP)]

    def scores(n, par):
        k0, q0 = place(n)
        for t in range(TQ // SUP):
            best = None
            for half in range(TK // SUP):
                s = lax.dot_general(
                    kall[pl.ds(k0 + half * SUP, SUP), :], qall[pl.ds(q0 + t * SUP, SUP), :],
                    (((1,), (1,)), ((), ())), preferred_element_type=jnp.float32,
                )
                S[par][half * SUP : (half + 1) * SUP, t * SUP : (t + 1) * SUP] = s
                for kb in range(4):
                    r = jnp.max(s[kb * TOK : (kb + 1) * TOK].reshape(TOK // 8, 8, SUP), axis=0)
                    r = jnp.where(kept(k0, q0, t, half * 4 + kb), r, LOW)
                    best = r if best is None else jnp.maximum(best, r)
            CM[par][:, t * SUP : (t + 1) * SUP] = best

    def weights(n, par):
        k0, q0 = place(n)
        qs = pl.ds(q0, TQ)
        old = mx[:, qs]
        new = jnp.maximum(old, jnp.max(CM[par][...], axis=0, keepdims=True))
        mx[:, qs] = new
        AL[par][...] = jnp.exp2((old - new) * SCALE)
        top = new * SCALE
        for t in range(TQ // SUP):
            ts = slice(t * SUP, (t + 1) * SUP)
            for kb in range(TK // TOK):
                less = jnp.where(kept(k0, q0, t, kb), top[:, ts], -LOW)
                ks = slice(kb * TOK, (kb + 1) * TOK)
                e = (S[par][ks, ts] * SCALE).reshape(TOK // 8, 8, SUP) - less[None]
                W[par][ks, ts] = jnp.exp2(e).reshape(TOK, SUP).astype(jnp.bfloat16)

    def sums(n, par):
        k0, q0 = place(n)
        for t in range(TQ // SUP):
            ts = slice(t * SUP, (t + 1) * SUP)
            qs = pl.ds(q0 + t * SUP, SUP)
            new = jnp.dot(vall[:, pl.ds(k0, TK)], W[par][:, ts], preferred_element_type=jnp.float32)
            acc[:, qs] = acc[:, qs] * AL[par][:1, ts] + new

    def stats(slot):
        at = slice(slot * SUP, (slot + 1) * SUP)
        m, l = mx[0:1, at], acc[DIM : DIM + 1, at]
        cut = [slice(b * TOK, (b + 1) * TOK) for b in range(4)]
        return jnp.concatenate([m[:, c] for c in cut] + [l[:, c] for c in cut], axis=0)

    def partial(slot, at):
        owner = group(slot)
        return (
            remote(osend.at[slot], orecv.at[at], o_s.at[slot, 0], o_r.at[at, 0], owner),
            remote(ssend.at[slot], srecv.at[at], o_s.at[slot, 1], o_r.at[at, 1], owner),
        )

    def send_partial(tile):
        for slot in (tile * 2 + 1, tile * 2):
            if slot > 0:
                osend[slot] = acc[0:DIM, slot * SUP : (slot + 1) * SUP].astype(jnp.bfloat16)
                ssend[slot] = stats(slot)
                for copy in partial(slot, BACK[slot]):
                    copy.start()

    queries_here(0)
    arrive(1, FRONT)
    give_all((4, 6, 5, 7))
    scores(jnp.int32(0), 0)
    p_b[...] = jnp.zeros_like(p_b)
    al_b[...] = jnp.ones_like(al_b)

    def before(n, parity):
        for at in range(parity, STEPS, 2):
            if at in RING_AT or at in QUERY_AT:

                @pl.when(n == at)
                def _(at=at):
                    for dist, whats in RING_AT.get(at, ()):
                        arrive(dist, whats)
                    if at in QUERY_AT:
                        queries_here(QUERY_AT[at])

    def after(n, parity):
        for at, tile in DONE_AT.items():
            if at % 2 == parity:

                @pl.when(n == at)
                def _(tile=tile):
                    send_partial(tile)

    def body(pair, carry):
        for par in range(2):
            n = 2 * pair + par
            before(n, par)
            scores(jnp.minimum(n + 1, STEPS - 1), 1 - par)
            weights(n, par)
            sums(jnp.maximum(n - 1, 0), 1 - par)
            after(n, par)
        return carry

    lax.fori_loop(0, STEPS // 2, body, 0)
    sums(jnp.int32(STEPS - 1), 1)
    send_partial(0)

    mine = stats(0)
    for slot in range(1, 8):
        for copy in partial(slot, slot):
            copy.wait_recv()
    all_stats = [mine] + [srecv[slot] for slot in range(1, 8)]
    best = functools.reduce(jnp.maximum, [st[0:4] for st in all_stats])
    factor = [jnp.exp2((st[0:4] - best) * SCALE) for st in all_stats]
    denom = functools.reduce(jnp.add, [st[4:8] * f for st, f in zip(all_stats, factor)])
    factor = [f / denom for f in factor]

    def home(block, x, c, at):
        return remote(fsend.at[block], frecv.at[at], f_s.at[block], f_r.at[at], device(x, c))

    for b in (2, 3, 0, 1):
        at = slice(b * TOK, (b + 1) * TOK)
        total = acc[0:DIM, at] * factor[0][b : b + 1]
        for slot in range(1, 8):
            total += orecv[slot, :, at].astype(jnp.float32) * factor[slot][b : b + 1]
        fsend[b] = total.T.astype(jnp.bfloat16)
        if b > 1:
            home(b, 1 - xl, b - 2, 2 + core).start()
    home(1 - core, xl, 1 - core, core).start()
    out_ref[:, head] = fsend[core]
    home(core, xl, 1 - core, 1 - core).wait_recv()
    out_ref[:, lanes(xl * 2 + 1 - core)] = frecv[1 - core]
    for c in range(2):
        home(2, 1 - xl, c, 2 + c).wait_recv()
        out_ref[:, lanes((1 - xl) * 2 + c)] = frecv[2 + c]

    for j in (1, 2, 3):
        for what in range(4):
            trade(j, what, mine_at[j]).wait_send()
    for b in (2, 3):
        home(b, 1 - xl, b - 2, 2 + core).wait_send()
    home(1 - core, xl, 1 - core, core).wait_send()
    for way in range(2):
        for dist in range(1, 5):
            for what in range(5):
                if goes(way, dist, what):
                    hop(way, dist, what).wait_send()
    for slot in range(1, 8):
        for copy in give(slot, BACK[slot]) + partial(slot, BACK[slot]):
            copy.wait_send()


def shards(queries, keys, values, block_pos):
    bf, f32, i32 = jnp.bfloat16, jnp.float32, jnp.int32
    vmem, dma = pltpu.VMEM, pltpu.SemaphoreType.DMA
    return pl.pallas_call(
        kernel,
        out_shape=jax.ShapeDtypeStruct(queries.shape, bf),
        in_specs=[pl.BlockSpec(memory_space=pl.ANY)] * 3 + [pl.BlockSpec(memory_space=pltpu.SMEM)],
        out_specs=pl.BlockSpec(memory_space=pltpu.VMEM),
        scratch_shapes=[
            vmem((NQ, DIM), bf), vmem((NK, DIM), bf), vmem((ROWS, NK), bf), vmem((8, NQ), i32), vmem((8, NK), i32),
            vmem((TOK, 4 * DIM), bf), vmem((4 * DIM, TOK), bf), vmem((8, TOK), i32), vmem((ROWS, NQ), f32), vmem((8, NQ), f32),
            vmem((8, TQ), f32), vmem((8, TQ), f32), vmem((8, TQ), f32), vmem((8, TQ), f32),
            vmem((TK, TQ), f32), vmem((TK, TQ), f32), vmem((TK, TQ), bf), vmem((TK, TQ), bf),
            vmem((8, DIM, SUP), bf), vmem((8, 8, TOK), f32), vmem((8, DIM, SUP), bf), vmem((8, 8, TOK), f32),
            vmem((4, TOK, DIM), bf), vmem((4, TOK, DIM), bf),
            dma((3,)), dma((3, 4)), dma((3, 4)), dma((2, 4, 5)), dma((2, 4, 5)), dma((8, 2)), dma((8, 2)), dma((8, 2)), dma((8, 2)),
            dma((4,)), dma((4,)),
        ],
        compiler_params=pltpu.CompilerParams(collective_id=0, has_side_effects=True, vmem_limit_bytes=56 << 20),
        cost_estimate=pl.CostEstimate(flops=NQ * NK * DIM * 4, bytes_accessed=1 << 20, transcendentals=NQ * NK),
        name="attend",
    )(queries, keys, values, block_pos)


def solution(mesh):
    spec = P(("outer", "inner"), None)
    return jax.shard_map(
        shards, mesh=mesh, in_specs=(spec, spec, spec, P(("outer", "inner"))), out_specs=spec, check_vma=False
    )
```

time: 81 us -> 70.9 us (0.88)
  Pallas kernels: 78.6 us -> 68.6 us
    pallas_call x1, Pallas kernels: 78.6 us -> 68.6 us  [shards(): pl.pallas_call(kernel, out_shape=jax.ShapeDtypeStruct(queries.shape, bf),...]
where the time goes in v2:
time: 70.9 us; the launch traced here: 70.8 us
  Pallas kernels  68.6 us (97%)
  local copies, waits for them, and re-layouts  1.57 us (2%)
    pallas_call x1, Pallas kernels, shards(): pl.pallas_call(kernel, out_shape=jax.ShapeDtypeStruct(queries.shape, bf),...  68.6 us
    unnamed x1, local copies, waits for them, and re-layouts  1.57 us

profile of v2, /device:TPU:1, one launch (start us, length us, event | category | flops | bytes accessed | tf_op | source)
XLA Modules:
  0.0 70.8 jit_solution(2713028717002444508)
XLA Ops:
  0.7 68.6 %attend.1 = bf16[128,512]{1,0:T(8,128)(2,1)} custom-call(bf16[128,512]{1,0:T(8,128)(2,1)} %q_in.1, bf16[128,512]{1,0:T(8,128)(2,1)} %k_in.1, bf16[128,512]{1,0:T(8,128)(2,1)} %v_in.1, s32[1]{0:T(128)S(6)} %copy.6.p_in), custom_call_target="tpu_custom_call" | custom-call | flops 8589934592 | bytes 1048576 | tf_op jit(solution)/shard_map/attend/pallas_call | solution.py:347
  69.3 1.6 %copy.7 = bf16[128,512]{1,0:T(8,128)(2,1)} copy(bf16[128,512]{1,0:T(8,128)(2,1)} %attend.1) | data formatting | bytes 262144

commit v3 on v2

--- a/solution.py
+++ b/solution.py
@@ -24,17 +24,17 @@
 
 OWN = 7
 K_A, V_A, K_B, V_B, POS = range(5)
-FRONT = (K_A, V_A, K_B, POS)
-RING_AT = {0: ((1, (3,)),), 1: ((2, (0, 1, 2, 4)),), 3: ((2, (3,)),), 5: ((3, (0, 1, 2, 4)),), 6: ((3, (3,)),), 9: ((4, (0, 1, 2, 4)),), 10: ((4, (3,)),)}
-QUERY_AT = {0: 1, 3: 2, 5: 3}
-DONE_AT = {14: 1, 12: 2, 11: 3}
+FRONT = (K_A, K_B, POS)
+RING_AT = {1: ((1, (1, 3)), (2, (0, 2, 4))), 3: ((2, (1, 3)),), 6: ((3, (0, 2, 4)),), 8: ((3, (1, 3)),), 9: ((4, (0, 2, 4)),), 11: ((4, (1, 3)),)}
+QUERY_AT = {0: 1, 3: 3, 4: 2}
+DONE_AT = {14: 1, 11: 3, 12: 2}
 TILES = NQ // TQ
 STEPS = (NK // TK) * TILES
 
 
 def kernel(
     q_in, k_in, v_in, p_in, out_ref,
-    qall, kall, vall, qpos, kpos, vin, vt, ptile, acc, mx,
+    qall, kall, vall, qpos, kpos, qcode, kcode, marks, vin, vt, ptile, acc, mx,
     cm_a, cm_b, al_a, al_b, s_a, s_b, p_a, p_b,
     osend, ssend, orecv, srecv, fsend, frecv,
     local, cell_s, cell_r, ring_s, ring_r, q_s, q_r, o_s, o_r, f_s, f_r,
@@ -78,8 +78,9 @@
     for load in loads:
         load.start()
     ptile[...] = jnp.full(ptile.shape, p_in[0], jnp.int32)
-    kpos[:, lanes(core, OWN * SUP)] = ptile[...]
-    vall[DIM:, :] = jnp.ones((ROWS - DIM, NK), jnp.bfloat16)
+    marks[core] = ptile[...]
+    vall[DIM:, 0:NK] = jnp.ones((ROWS - DIM, NK), jnp.bfloat16)
+    vall[:, NK:] = jnp.zeros((ROWS, TK), jnp.bfloat16)
     for load in loads:
         load.wait()
     for h in range(4):
@@ -93,7 +94,7 @@
             (k_in.at[:, lanes(to)], kall.at[lanes(block, OWN * SUP), :]),
             (vt.at[lanes(to), :], vall.at[pl.ds(0, DIM), lanes(block, OWN * SUP)]),
             (q_in.at[:, lanes(to)], qall.at[lanes(block), :]),
-            (ptile, kpos.at[:, lanes(block, OWN * SUP)]),
+            (ptile, marks.at[block]),
         )[what]
         return remote(src, dst, cell_s.at[j - 1, what], cell_r.at[j - 1, what], device(x, c))
 
@@ -116,8 +117,13 @@
         elif what in (V_A, V_B):
             refs = vall.at[0:DIM, a], vall.at[0:DIM, b]
         else:
-            refs = kpos.at[:, a], kpos.at[:, b]
+            refs = kcode.at[src], kcode.at[dst]
         return remote(*refs, ring_s.at[way, dist - 1, what], ring_r.at[way, dist - 1, what], ring(1 if way == 0 else 7))
+
+    def spread(wide, slot, code):
+        for b in range(4):
+            at = slice(slot * SUP + b * TOK, slot * SUP + (b + 1) * TOK)
+            wide[:, at] = jnp.broadcast_to(code[slot, b : b + 1, :], (8, TOK))
 
     def goes(way, dist, what):
         return dist < 4 or (dist == 4 and (what in (V_A, V_B)) == (way == 1))
@@ -129,13 +135,22 @@
                     hop(way, dist, what).wait_recv()
                     if goes(way, dist + 1, what):
                         hop(way, dist + 1, what).start()
+                    if what == POS:
+                        spread(kpos, 6 if dist == 4 else 2 * (dist - 1) + way, kcode)
 
     def give(slot, at):
         a, b = slice(0, SUP), slice(at * SUP, (at + 1) * SUP)
-        ka = slice(OWN * SUP, (OWN + 1) * SUP)
         return (
             remote(qall.at[a, :], qall.at[b, :], q_s.at[slot, 0], q_r.at[at, 0], group(slot)),
-            remote(kpos.at[:, ka], qpos.at[:, b], q_s.at[slot, 1], q_r.at[at, 1], group(slot)),
+            remote(kcode.at[OWN], qcode.at[at], q_s.at[slot, 1], q_r.at[at, 1], group(slot)),
+        )
+
+    def pass_on(slot):
+        at = 4 + BACK[slot]
+        a, b = slice(4 * SUP, 5 * SUP), slice(at * SUP, (at + 1) * SUP)
+        return (
+            remote(qall.at[a, :], qall.at[b, :], q_s.at[4 + slot, 0], q_r.at[at, 0], group(slot)),
+            remote(qcode.at[4], qcode.at[at], q_s.at[4 + slot, 1], q_r.at[at, 1], group(slot)),
         )
 
     def give_all(slots):
@@ -153,22 +168,27 @@
 
     traded(0, (1,))
     send_on(K_A)
+    traded(3, (1, 2, 3))
+    row = lax.broadcasted_iota(jnp.int32, (8, TOK), 0)
+    kcode[OWN] = jnp.where(row == 0, marks[0], jnp.where(row == 1, marks[1], jnp.where(row == 2, marks[2], marks[3])))
+    send_on(POS)
+    spread(kpos, OWN, kcode)
+    traded(0, (2, 3))
+    send_on(K_B)
     traded(1, (1,))
     send_on(V_A)
-    traded(3, (1, 2, 3))
-    send_on(POS)
-    traded(0, (2, 3))
-    send_on(K_B)
     traded(2, (1, 2, 3))
-    give_all((2, 1, 3))
+    give_all((4, 2, 1, 3))
     traded(1, (2, 3))
     send_on(V_B)
 
     def queries_here(tile):
         for slot in range(tile * 2, tile * 2 + 2):
-            if slot > 0:
+            if slot not in (0, 4):
                 for copy in give(slot, slot):
                     copy.wait_recv()
+            if slot > 0:
+                spread(qpos, slot, qcode)
 
     qpos[:, 0:SUP] = kpos[:, OWN * SUP :]
     acc[:, SUP:] = jnp.zeros((ROWS, NQ - SUP), jnp.float32)
@@ -178,17 +198,17 @@
         at = slice(b * TOK, (b + 1) * TOK)
         kat = slice(OWN * SUP + b * TOK, OWN * SUP + (b + 1) * TOK)
         s = lax.dot_general(kall[kat, :], qall[at, :], (((1,), (1,)), ((), ())), preferred_element_type=jnp.float32)
-        s = jnp.where(causal, s, LOW)
+        s = jnp.where(causal, s * SCALE, LOW)
         top = jnp.max(s, axis=0, keepdims=True)
-        w = jnp.where(causal, jnp.exp2(s * SCALE - top * SCALE), 0.0).astype(jnp.bfloat16)
+        w = jnp.where(causal, jnp.exp2(s - top), 0.0).astype(jnp.bfloat16)
         acc[:, at] = jnp.dot(vall[:, kat], w, preferred_element_type=jnp.float32)
         mx[:, at] = jnp.broadcast_to(top, (8, TOK))
 
     S, W, CM, AL = (s_a, s_b), (p_a, p_b), (cm_a, cm_b), (al_a, al_b)
 
     def place(n):
-        keys = jnp.where(n < 2, 0, jnp.where(n < 4, 1, jnp.where(n < 5, 0, jnp.where(n < 6, 1, jnp.where(n < 7, 0, jnp.where(n < 8, 1, jnp.where(n < 10, 2, jnp.where(n < 12, 3, jnp.where(n < 13, 2, jnp.where(n < 14, 3, jnp.where(n < 15, 2, 3)))))))))))
-        tile = jnp.where(n < 1, 0, jnp.where(n < 2, 1, jnp.where(n < 3, 0, jnp.where(n < 4, 1, jnp.where(n < 6, 2, jnp.where(n < 9, 3, jnp.where(n < 10, 2, jnp.where(n < 11, 3, jnp.where(n < 12, 2, jnp.where(n < 14, 1, 0))))))))))
+        keys = jnp.where(n < 2, 0, jnp.where(n < 4, 1, jnp.where(n < 6, 0, jnp.where(n < 8, 1, jnp.where(n < 10, 2, jnp.where(n < 12, 3, jnp.where(n < 13, 2, jnp.where(n < 14, 3, jnp.where(n < 15, 2, 3)))))))))
+        tile = jnp.where(n < 1, 0, jnp.where(n < 2, 1, jnp.where(n < 3, 0, jnp.where(n < 4, 1, jnp.where(n < 5, 3, jnp.where(n < 6, 2, jnp.where(n < 7, 3, jnp.where(n < 8, 2, jnp.where(n < 9, 3, jnp.where(n < 10, 2, jnp.where(n < 11, 3, jnp.where(n < 12, 2, jnp.where(n < 14, 1, 0)))))))))))))
         return pl.multiple_of(keys * TK, TK), pl.multiple_of(tile * TQ, TQ)
 
     def kept(k0, q0, t, kb):
@@ -203,7 +223,7 @@
                 s = lax.dot_general(
                     kall[pl.ds(k0 + half * SUP, SUP), :], qall[pl.ds(q0 + t * SUP, SUP), :],
                     (((1,), (1,)), ((), ())), preferred_element_type=jnp.float32,
-                )
+                ) * SCALE
                 S[par][half * SUP : (half + 1) * SUP, t * SUP : (t + 1) * SUP] = s
                 for kb in range(4):
                     r = jnp.max(s[kb * TOK : (kb + 1) * TOK].reshape(TOK // 8, 8, SUP), axis=0)
@@ -217,18 +237,18 @@
         old = mx[:, qs]
         new = jnp.maximum(old, jnp.max(CM[par][...], axis=0, keepdims=True))
         mx[:, qs] = new
-        AL[par][...] = jnp.exp2((old - new) * SCALE)
-        top = new * SCALE
+        AL[par][...] = jnp.exp2(old - new)
         for t in range(TQ // SUP):
             ts = slice(t * SUP, (t + 1) * SUP)
             for kb in range(TK // TOK):
-                less = jnp.where(kept(k0, q0, t, kb), top[:, ts], -LOW)
+                less = jnp.where(kept(k0, q0, t, kb), new[:, ts], -LOW)
                 ks = slice(kb * TOK, (kb + 1) * TOK)
-                e = (S[par][ks, ts] * SCALE).reshape(TOK // 8, 8, SUP) - less[None]
+                e = S[par][ks, ts].reshape(TOK // 8, 8, SUP) - less[None]
                 W[par][ks, ts] = jnp.exp2(e).reshape(TOK, SUP).astype(jnp.bfloat16)
 
     def sums(n, par):
-        k0, q0 = place(n)
+        k0, q0 = place(jnp.maximum(n, 0))
+        k0 = pl.multiple_of(jnp.where(n < 0, NK, k0), TK)
         for t in range(TQ // SUP):
             ts = slice(t * SUP, (t + 1) * SUP)
             qs = pl.ds(q0 + t * SUP, SUP)
@@ -257,8 +277,12 @@
                     copy.start()
 
     queries_here(0)
+    for copy in give(4, 4):
+        copy.wait_recv()
+    for slot in (1, 3, 2):
+        for copy in pass_on(slot):
+            copy.start()
     arrive(1, FRONT)
-    give_all((4, 6, 5, 7))
     scores(jnp.int32(0), 0)
     p_b[...] = jnp.zeros_like(p_b)
     al_b[...] = jnp.ones_like(al_b)
@@ -288,7 +312,7 @@
             before(n, par)
             scores(jnp.minimum(n + 1, STEPS - 1), 1 - par)
             weights(n, par)
-            sums(jnp.maximum(n - 1, 0), 1 - par)
+            sums(n - 1, 1 - par)
             after(n, par)
         return carry
 
@@ -302,7 +326,7 @@
             copy.wait_recv()
     all_stats = [mine] + [srecv[slot] for slot in range(1, 8)]
     best = functools.reduce(jnp.maximum, [st[0:4] for st in all_stats])
-    factor = [jnp.exp2((st[0:4] - best) * SCALE) for st in all_stats]
+    factor = [jnp.exp2(st[0:4] - best) for st in all_stats]
     denom = functools.reduce(jnp.add, [st[4:8] * f for st, f in zip(all_stats, factor)])
     factor = [f / denom for f in factor]
 
@@ -337,7 +361,7 @@
                 if goes(way, dist, what):
                     hop(way, dist, what).wait_send()
     for slot in range(1, 8):
-        for copy in give(slot, BACK[slot]) + partial(slot, BACK[slot]):
+        for copy in (give(slot, BACK[slot]) if slot < 5 else pass_on(slot - 4)) + partial(slot, BACK[slot]):
             copy.wait_send()
 
 
@@ -350,7 +374,7 @@
         in_specs=[pl.BlockSpec(memory_space=pl.ANY)] * 3 + [pl.BlockSpec(memory_space=pltpu.SMEM)],
         out_specs=pl.BlockSpec(memory_space=pltpu.VMEM),
         scratch_shapes=[
-            vmem((NQ, DIM), bf), vmem((NK, DIM), bf), vmem((ROWS, NK), bf), vmem((8, NQ), i32), vmem((8, NK), i32),
+            vmem((NQ, DIM), bf), vmem((NK, DIM), bf), vmem((ROWS, NK + TK), bf), vmem((8, NQ), i32), vmem((8, NK), i32), vmem((8, 8, TOK), i32), vmem((8, 8, TOK), i32), vmem((4, 8, TOK), i32),
             vmem((TOK, 4 * DIM), bf), vmem((4 * DIM, TOK), bf), vmem((8, TOK), i32), vmem((ROWS, NQ), f32), vmem((8, NQ), f32),
             vmem((8, TQ), f32), vmem((8, TQ), f32), vmem((8, TQ), f32), vmem((8, TQ), f32),
             vmem((TK, TQ), f32), vmem((TK, TQ), f32), vmem((TK, TQ), bf), vmem((TK, TQ), bf),

time: 70.9 us -> 67.6 us (0.953)
  Pallas kernels: 68.6 us -> 65.3 us
    pallas_call x1, Pallas kernels: 68.6 us -> 65.3 us  [shards(): pl.pallas_call(kernel, out_shape=jax.ShapeDtypeStruct(queries.shape, bf),...]
where the time goes in v3:
time: 67.6 us; the launch traced here: 67.5 us
  Pallas kernels  65.3 us (97%)
  local copies, waits for them, and re-layouts  1.57 us (2%)
    pallas_call x1, Pallas kernels, shards(): pl.pallas_call(kernel, out_shape=jax.ShapeDtypeStruct(queries.shape, bf),...  65.3 us
    unnamed x1, local copies, waits for them, and re-layouts  1.57 us

profile of v3, /device:TPU:1, one launch (start us, length us, event | category | flops | bytes accessed | tf_op | source)
XLA Modules:
  0.0 67.5 jit_solution(14625897224135704821)
XLA Ops:
  0.7 65.3 %attend.1 = bf16[128,512]{1,0:T(8,128)(2,1)} custom-call(bf16[128,512]{1,0:T(8,128)(2,1)} %q_in.1, bf16[128,512]{1,0:T(8,128)(2,1)} %k_in.1, bf16[128,512]{1,0:T(8,128)(2,1)} %v_in.1, s32[1]{0:T(128)S(6)} %copy.6.p_in), custom_call_target="tpu_custom_call" | custom-call | flops 8589934592 | bytes 1048576 | tf_op jit(solution)/shard_map/attend/pallas_call | solution.py:371
  66.0 1.6 %copy.7 = bf16[128,512]{1,0:T(8,128)(2,1)} copy(bf16[128,512]{1,0:T(8,128)(2,1)} %attend.1) | data formatting | bytes 262144

commit v4 on v3

--- a/solution.py
+++ b/solution.py
@@ -310,9 +310,9 @@
         for par in range(2):
             n = 2 * pair + par
             before(n, par)
-            scores(jnp.minimum(n + 1, STEPS - 1), 1 - par)
             weights(n, par)
             sums(n - 1, 1 - par)
+            scores(jnp.minimum(n + 1, STEPS - 1), 1 - par)
             after(n, par)
         return carry
 

time: 67.6 us -> 65.7 us (0.972)
  Pallas kernels: 65.3 us -> 63.3 us
    pallas_call x1, Pallas kernels: 65.3 us -> 63.3 us  [shards(): pl.pallas_call(kernel, out_shape=jax.ShapeDtypeStruct(queries.shape, bf),...]
where the time goes in v4:
time: 65.7 us; the launch traced here: 65.5 us
  Pallas kernels  63.3 us (96%)
  local copies, waits for them, and re-layouts  1.57 us (2%)
  between operations  0.66 us (1%)
    pallas_call x1, Pallas kernels, shards(): pl.pallas_call(kernel, out_shape=jax.ShapeDtypeStruct(queries.shape, bf),...  63.3 us
    unnamed x1, local copies, waits for them, and re-layouts  1.57 us

profile of v4, /device:TPU:1, one launch (start us, length us, event | category | flops | bytes accessed | tf_op | source)
XLA Modules:
  0.0 65.5 jit_solution(4536832006879922256)
XLA Ops:
  0.7 63.3 %attend.1 = bf16[128,512]{1,0:T(8,128)(2,1)} custom-call(bf16[128,512]{1,0:T(8,128)(2,1)} %q_in.1, bf16[128,512]{1,0:T(8,128)(2,1)} %k_in.1, bf16[128,512]{1,0:T(8,128)(2,1)} %v_in.1, s32[1]{0:T(128)S(6)} %copy.6.p_in), custom_call_target="tpu_custom_call" | custom-call | flops 8589934592 | bytes 1048576 | tf_op jit(solution)/shard_map/attend/pallas_call | solution.py:371
  64.0 1.6 %copy.7 = bf16[128,512]{1,0:T(8,128)(2,1)} copy(bf16[128,512]{1,0:T(8,128)(2,1)} %attend.1) | data formatting | bytes 262144
